TPU v7x, 32 devices: a whole 2x2x4 slice. The times are simulated.
32 devices in a mesh: dp: 8 (over z, x), mp: 4 (over y, core).
Axes of the slice: x: 2, y: 2, z: 4, core: 2. Of those that a mesh axis runs over, the one named last changes fastest.
Arguments:
- attn: bfloat16 [2, 512, 2048], P(None, 'dp', 'mp'), may hold values from -6 to 6
- resid: bfloat16 [2, 512, 4096], P(None, 'dp', 'mp'), may hold values from -6 to 6
- w_out: bfloat16 [4096, 2048], P('dp', 'mp'), may hold values from -0.125 to 0.125
- gain: float32 [4096], P('mp'), may hold values from 0.1 to 1.9
- neg_owner: int32 [512, 31], P('dp'), may hold values from 0 to 7, as said below
- neg_local: int32 [512, 31], P('dp'), may hold values from 0 to 63
Outputs:
- attn_grad: bfloat16 [2, 512, 2048], P(None, 'dp', 'mp')
- weight_grad: float32 [4096, 2048], P('dp', 'mp')
- gain_grad: float32 [4096], P('mp')
Inputs may be any that keep to these rules, and one draw needn't show every extreme that they name: `neg_owner`: among the 64 queries of one index of dp (aligned blocks of rows), no owner is named more than 496 times, and some owner exactly 496 times.
All inputs are finite; a program needn't handle non-finite values.
Results may differ from a plain program's by a relative error of at most 0.0052.
Values may be sent and summed in bfloat16 or wider, within the bound.
A program may use at most 128 MiB of HBM per device.

v0:
```python
import jax
import jax.numpy as jnp
from jax import lax
from jax.sharding import PartitionSpec as P

TAU = 0.05
LOSS_SCALE = 32.0
EPS = 1e-06


def shards(attn, resid, w_out, gain, neg_owner, neg_local):
    groups = lax.axis_size("dp")
    pairs_here = attn.shape[1]
    feats = resid.shape[2]
    neg_count = neg_owner.shape[1]
    capacity = 2 * pairs_here * neg_count // groups
    rows_a = attn.reshape(2 * pairs_here, attn.shape[2])
    weight_full = lax.all_gather(w_out, "dp", axis=0, tiled=True)
    proj_part = lax.dot_general(
        rows_a, weight_full, (((1,), (1,)), ((), ())), preferred_element_type=jnp.float32
    )
    proj = lax.psum_scatter(proj_part, "mp", scatter_dimension=1, tiled=True)
    hidden = resid.reshape(2 * pairs_here, feats).astype(jnp.float32) + proj
    normed = hidden * gain
    squares = lax.psum(jnp.sum(normed * normed, axis=1), "mp")
    recip = lax.rsqrt(squares + EPS)[:, None]
    emb = (normed * recip).astype(jnp.bfloat16)
    query = emb[:pairs_here]
    docs = emb[pairs_here:]
    flat_owner = neg_owner.reshape(-1)
    flat_local = neg_local.reshape(-1)
    onehot = (flat_owner[:, None] == jnp.arange(groups, dtype=jnp.int32)[None, :]).astype(jnp.int32)
    ranks = jnp.sum((jnp.cumsum(onehot, axis=0) - 1) * onehot, axis=1)
    slot = flat_owner * capacity + ranks
    request = jnp.full((groups * capacity,), -1, jnp.int32).at[slot].set(flat_local)
    asked = lax.all_to_all(
        request.reshape(groups, capacity), "dp", split_axis=0, concat_axis=0, tiled=True
    )
    valid = asked >= 0
    safe_rows = jnp.maximum(asked, 0)
    outgoing = jnp.where(valid[:, :, None], docs[safe_rows], jnp.zeros((), jnp.bfloat16))
    fetched = lax.all_to_all(outgoing, "dp", split_axis=0, concat_axis=0, tiled=True)
    neg_emb = fetched.reshape(groups * capacity, feats)[slot].reshape(pairs_here, neg_count, feats)
    pos_part = jnp.sum(query.astype(jnp.float32) * docs.astype(jnp.float32), axis=1)
    neg_part = jnp.einsum("pd,pkd->pk", query, neg_emb, preferred_element_type=jnp.float32)
    partial_value = jnp.concatenate([pos_part[:, None], neg_part], axis=1)
    scores = lax.psum(partial_value, "mp") / TAU
    expo = jnp.exp(scores)
    prob = expo / jnp.sum(expo, axis=1, keepdims=True)
    first = (jnp.arange(neg_count + 1) == 0).astype(jnp.float32)[None, :]
    wts = LOSS_SCALE * (prob - first) / TAU
    query_f = query.astype(jnp.float32)
    grad_query = wts[:, 0:1] * docs.astype(jnp.float32) + jnp.einsum(
        "pk,pkd->pd", wts[:, 1:], neg_emb, preferred_element_type=jnp.float32
    )
    terms = (wts[:, 1:, None] * query_f[:, None, :]).astype(jnp.bfloat16)
    slot_buffer = (
        jnp.zeros((groups * capacity, feats), jnp.bfloat16).at[slot].set(terms.reshape(-1, feats))
    )
    returned = lax.all_to_all(
        slot_buffer.reshape(groups, capacity, feats), "dp", split_axis=0, concat_axis=0, tiled=True
    )
    targets = jnp.where(valid, asked, pairs_here).reshape(-1)
    selector = (jnp.arange(pairs_here, dtype=jnp.int32)[:, None] == targets[None, :]).astype(
        jnp.bfloat16
    )
    grad_docs = wts[:, 0:1] * query_f + jnp.dot(
        selector, returned.reshape(-1, feats), preferred_element_type=jnp.float32
    )
    demb = jnp.concatenate([grad_query, grad_docs], axis=0)
    inner = lax.psum(jnp.sum(normed * demb, axis=1), "mp")[:, None]
    dnorm = recip * demb - recip * recip * recip * normed * inner
    gain_grad = lax.psum(jnp.sum(dnorm * hidden, axis=0), "dp")
    dh = (dnorm * gain).astype(jnp.bfloat16)
    dh_full = lax.all_gather(dh, "mp", axis=1, tiled=True)
    attn_grad = (
        jnp.dot(dh_full, weight_full, preferred_element_type=jnp.float32)
        .astype(jnp.bfloat16)
        .reshape(attn.shape)
    )
    weight_grad = lax.psum_scatter(
        lax.dot_general(
            dh_full, rows_a, (((0,), (0,)), ((), ())), preferred_element_type=jnp.float32
        ),
        "dp",
        scatter_dimension=0,
        tiled=True,
    )
    return (attn_grad, weight_grad, gain_grad)


def solution(mesh):
    in_specs = (
        P(None, "dp", "mp"),
        P(None, "dp", "mp"),
        P("dp", "mp"),
        P("mp"),
        P("dp", None),
        P("dp", None),
    )
    out_specs = (P(None, "dp", "mp"), P("dp", "mp"), P("mp"))
    return jax.shard_map(shards, mesh=mesh, in_specs=in_specs, out_specs=out_specs, check_vma=False)
```

profile of v0, /device:TPU:0, one launch (start us, length us, event | category | flops | bytes accessed | tf_op | source)
XLA Modules:
  0.0 761.4 jit_solution(12199494173355422516)
XLA Ops:
  7.3 0.7 all-gather.3.cloned.1.call-update
  8.0 78.3 %all-gather.3.cloned.1.call-done = bf16[4096,512]{1,0:T(8,128)(2,1)} async-done(((bf16[512,512]{1,0:T(8,128)(2,1)}), bf16[4096,512]{1,0:T(8,128)(2,1)}) %all-gather.3.cloned.1.call-update) | async-done | bytes 4194320 | tf_op jit(solution)/shard_map/all_gather | solution.py:18
  86.3 5.0 fusion.13
  92.1 2.3 reduce-window.6
  95.1 10.0 %scatter_custom_fusion = s32[3968]{0:T(1024)S(1)} fusion(s32[1984]{0:T(1024)S(1)} %bitcast.71, s32[1984]{0:T(1024)S(1)} %reshape.152, s32[]{:T(128)} %constant.13.clone.1), kind=kCustom, calls=%fused_computation.51 | custom fusion | bytes 15876 | tf_op jit(solution)/shard_map/scatter | solution.py:35
  105.1 9.2 %all_to_all.22 = s32[8,1,496]{2,1,0:T(1,128)S(1)} all-to-all(s32[8,1,496]{2,1,0:T(1,128)S(1)} %all_to_all.14), channel_id=1, replica_groups=mesh['dp'=8,'mp'=4] {'dp'}, dimensions={0} | all-to-all | bytes 31744 | tf_op jit(solution)/shard_map/all_to_all | solution.py:36
  114.5 6.8 reduce-scatter.3.cloned.1.call-done
  121.3 1.2 multiply_reduce_fusion.2
  122.5 5.8 psum.28
  128.3 1.1 multiply_convert_fusion.3
  129.4 13.3 %gather_fusion = bf16[3968,1024]{1,0:T(8,128)(2,1)} fusion(bf16[64,1024]{1,0:T(8,128)(2,1)S(1)} %get-tuple-element.6, s32[4096]{0:T(1024)S(1)} %pad_clamp_fusion), kind=kCustom, calls=%fused_computation | custom fusion | bytes 16268800 | tf_op jit(solution)/shard_map/gather | solution.py:41
  142.8 7.4 broadcast_select_fusion
  150.2 5.7 all-to-all-start.1
  156.1 4.3 mul.135
  160.4 7.2 mul.136
  167.5 165.7 %all-to-all-done.1 = bf16[8,496,1024]{2,1,0:T(8,128)(2,1)} async-done(((bf16[8,496,1024]{2,1,0:T(8,128)(2,1)}), bf16[8,496,1024]{2,1,0:T(8,128)(2,1)}, u32[]{:S(2)}, u32[]{:S(2)}) %all-to-all-start.1) | async-done | bytes 8126496 | tf_op jit(solution)/shard_map/all_to_all | solution.py:42
  333.2 15.3 %gather_fusion.1 = bf16[1984,1024]{1,0:T(8,128)(2,1)} fusion(bf16[3968,1024]{1,0:T(8,128)(2,1)} %bitcast.9, s32[2048]{0:T(1024)S(1)} %pad_clamp_fusion.1), kind=kCustom, calls=%fused_computation.1 | custom fusion | bytes 8134400 | tf_op jit(solution)/shard_map/gather | solution.py:43
  348.5 5.1 reshape.126
  353.6 3.4 fusion.6
  357.1 10.4 %psum.29 = f32[64,32]{1,0:T(8,128)S(1)} all-reduce(f32[64,32]{1,0:T(8,128)S(1)} %pad_maximum_fusion.1), channel_id=1, replica_groups=mesh['dp'=8,'mp'=4] {'mp'}, use_global_device_ids=true, to_apply=%region_8.9 | all-reduce | flops 2048 | bytes 16384 | tf_op jit(solution)/shard_map/psum | solution.py:47
  368.0 22.3 %scatter_custom_fusion.1 = bf16[3968,1024]{1,0:T(8,128)(2,1)} fusion(s32[1984]{0:T(1024)S(1)} %bitcast.73, f32[1984,1024]{1,0:T(8,128)} %mul.136, f32[1984]{0:T(1024)S(1)} %mul.133, bf16[]{:T(256)} %constant.10.clone.1), kind=kCustom, calls=%fused_computation.6 | custom fusion | flops 4063232 | bytes 16261122 | tf_op jit(solution)/shard_map/scatter | solution.py:58
  390.2 5.0 all-to-all-start.2
  395.5 2.9 fusion.14
  398.5 174.1 %all-to-all-done.2 = bf16[8,496,1024]{2,1,0:T(8,128)(2,1)} async-done(((bf16[8,496,1024]{2,1,0:T(8,128)(2,1)}), bf16[8,496,1024]{2,1,0:T(8,128)(2,1)}, u32[]{:S(2)}, u32[]{:S(2)}) %all-to-all-start.2) | async-done | bytes 8126496 | tf_op jit(solution)/shard_map/all_to_all | solution.py:60
  572.7 4.8 convolution_add_fusion
  577.7 5.7 psum.30
  583.4 0.9 multiply_reduce_fusion
  584.4 16.1 %all-gather.5.cloned.1.call-done = bf16[128,4096]{1,0:T(8,128)(2,1)} async-done(((bf16[128,1024]{1,0:T(8,128)(2,1)}), bf16[128,4096]{1,0:T(8,128)(2,1)}) %all-gather.5.cloned.1.call-update) | async-done | bytes 1048592 | tf_op jit(solution)/shard_map/all_gather | solution.py:75
  600.5 5.8 fusion.15
  606.3 22.3 %psum.31 = f32[1024]{0:T(1024)} all-reduce(f32[1024]{0:T(1024)S(1)} %get-tuple-element.3), channel_id=1, replica_groups=mesh['dp'=8,'mp'=4] {'dp'}, use_global_device_ids=true, to_apply=%region_15.16 | all-reduce | flops 1024 | bytes 8192 | tf_op jit(solution)/shard_map/psum | solution.py:73
  628.6 3.6 convolution_convert_fusion
  632.2 122.6 %reduce-scatter.5.cloned.1.call-done = f32[512,512]{1,0:T(8,128)} async-done(((f32[4096,512]{1,0:T(8,128)}), f32[512,512]{1,0:T(8,128)}) %reduce-scatter.5.cloned.1.call-update) | async-done | bytes 1048592 | tf_op jit(solution)/shard_map/reduce_scatter | solution.py:81
  (59 shorter events, 3.1 us)
Async XLA Ops:
  7.2 79.1 %copy-start = (bf16[2,64,512]{2,1,0:T(8,128)(2,1)S(1)}, bf16[2,64,512]{2,1,0:T(8,128)(2,1)}, u32[]{:S(2)}) copy-start(bf16[2,64,512]{2,1,0:T(8,128)(2,1)} %param.6) | copy-start | bytes 393220
  7.2 84.2 %copy-start.5 = (s32[64,31]{0,1:T(8,128)S(1)}, s32[64,31]{0,1:T(8,128)}, u32[]{:S(2)}) copy-start(s32[64,31]{0,1:T(8,128)} %param.10) | copy-start | bytes 23812
  7.2 84.5 %copy-start.6 = (s32[64,31]{0,1:T(8,128)S(1)}, s32[64,31]{0,1:T(8,128)}, u32[]{:S(2)}) copy-start(s32[64,31]{0,1:T(8,128)} %param.11) | copy-start | bytes 23812
  7.2 114.1 %copy-start.4 = (f32[1024]{0:T(1024)S(1)}, f32[1024]{0:T(1024)}, u32[]{:S(2)}) copy-start(f32[1024]{0:T(1024)} %param.9) | copy-start | bytes 12292
  7.2 114.1 %copy-start.3 = (bf16[2,64,1024]{2,1,0:T(8,128)(2,1)S(1)}, bf16[2,64,1024]{2,1,0:T(8,128)(2,1)}, u32[]{:S(2)}) copy-start(bf16[2,64,1024]{2,1,0:T(8,128)(2,1)} %param.7) | copy-start | bytes 786436
  7.2 79.1 %all-gather.3.cloned.1.call-start = ((), (), s32[]{:S(2)}) async-start(), calls=%async_computation.5 | async-start | bytes 4718592 | tf_op jit(solution)/shard_map/all_gather | solution.py:18
  8.0 113.3 %reduce-scatter.3.cloned.1.call-start = ((), (), s32[]{:S(2)}) async-start(), calls=%async_computation.6 | async-start | bytes 2621440 | tf_op jit(solution)/shard_map/reduce_scatter | solution.py:22
  150.2 183.0 %all-to-all-start.1 = ((bf16[8,496,1024]{2,1,0:T(8,128)(2,1)}), bf16[8,496,1024]{2,1,0:T(8,128)(2,1)}, u32[]{:S(2)}, u32[]{:S(2)}) async-start(bf16[8,496,1024]{2,1,0:T(8,128)(2,1)} %broadcast_select_fusion), calls=%async_computation.2 | async-start | bytes 16252928 | tf_op jit(solution)/shard_map/all_to_all | solution.py:42
  390.2 182.4 %all-to-all-start.2 = ((bf16[8,496,1024]{2,1,0:T(8,128)(2,1)}), bf16[8,496,1024]{2,1,0:T(8,128)(2,1)}, u32[]{:S(2)}, u32[]{:S(2)}) async-start(bf16[8,496,1024]{2,1,0:T(8,128)(2,1)} %bitcast.64), calls=%async_computation.3 | async-start | bytes 16252928 | tf_op jit(solution)/shard_map/all_to_all | solution.py:60
  395.2 205.2 %all-gather.5.cloned.1.call-start = ((), (), s32[]{:S(2)}) async-start(), calls=%async_computation.7 | async-start | bytes 1310720 | tf_op jit(solution)/shard_map/all_gather | solution.py:75
  398.5 179.0 %copy-start.1 = (f32[128,1024]{1,0:T(8,128)S(1)}, f32[128,1024]{1,0:T(8,128)}, u32[]{:S(2)}) copy-start(f32[128,1024]{1,0:T(8,128)} %reduce-scatter.3.cloned.1.call-done) | copy-start | bytes 1572868
  584.3 170.5 %reduce-scatter.5.cloned.1.call-start = ((), (), s32[]{:S(2)}) async-start(), calls=%async_computation.8 | async-start | bytes 9437184 | tf_op jit(solution)/shard_map/reduce_scatter | solution.py:81
  600.5 28.1 %copy-start.2 = (bf16[128,4096]{1,0:T(8,128)(2,1)S(1)}, bf16[128,4096]{1,0:T(8,128)(2,1)}, u32[]{:S(2)}) copy-start(bf16[128,4096]{1,0:T(8,128)(2,1)} %all-gather.5.cloned.1.call-done) | copy-start | bytes 3145732
Sparse Core Ops, SparseCore 0:
  10.2 76.0 all-gather.2
  91.5 29.7 reduce-scatter.2
  584.4 15.9 all-gather.4
  606.4 148.3 reduce-scatter.4
where the time goes:
time: 762 us; the launch traced here: 761 us
  waiting for transfers between devices  564 us (74%)
  local copies, waits for them, and re-layouts  56.9 us (7%)
  blocking collectives  53.4 us (7%)
  other arithmetic  36.4 us (5%)
  matrix products  25.5 us (3%)
  between operations  14.1 us (2%)
  starting transfers between devices  10.8 us (1%)
    all_to_all x1, waiting for transfers between devices, shards(): lax.all_to_all(slot_buffer.reshape(groups, capacity, feats), 'dp', split_...  174 us
    all_to_all x1, waiting for transfers between devices, shards(): lax.all_to_all(outgoing, 'dp', split_axis=0, concat_axis=0, tiled=True)  166 us
    reduce_scatter x1, waiting for transfers between devices, shards(): lax.psum_scatter(lax.dot_general(dh_full, rows_a, (((0,), (0,)), ((), ())...  123 us
    all_gather x1, waiting for transfers between devices, shards(): weight_full = lax.all_gather(w_out, 'dp', axis=0, tiled=True)  78.3 us
    scatter x1, other arithmetic, shards(): jnp.zeros((groups * capacity, feats), jnp.bfloat16).at[slot]  22.3 us
    psum x1, blocking collectives, shards(): gain_grad = lax.psum(jnp.sum(dnorm * hidden, axis=0), 'dp')  22.3 us
    all_gather x1, waiting for transfers between devices, shards(): dh_full = lax.all_gather(dh, 'mp', axis=1, tiled=True)  16.1 us
    gather x1, local copies, waits for them, and re-layouts, shards(): fetched.reshape(groups * capacity, feats)[slot]  15.3 us
  transfers between devices with their start and end apart: 6, of which 6 were waited for; matrix products, arithmetic and copies ran while one was open for 4% of the time, Pallas kernels for 0%

commit v1 on v0

--- a/solution.py
+++ b/solution.py
@@ -8,7 +8,7 @@
 EPS = 1e-06
 
 
-def shards(attn, resid, w_out, gain, neg_owner, neg_local):
+def by_query(attn, resid, w_out, gain, neg_owner, neg_local):
     groups = lax.axis_size("dp")
     pairs_here = attn.shape[1]
     feats = resid.shape[2]
@@ -89,6 +89,107 @@
     return (attn_grad, weight_grad, gain_grad)
 
 
+def by_feature(attn, resid, w_out, gain, neg_owner, neg_local):
+    groups, quarters = lax.axis_size("dp"), lax.axis_size("mp")
+    d, m = lax.axis_index("dp"), lax.axis_index("mp")
+    pairs_here = attn.shape[1]
+    rows_here = 2 * pairs_here
+    pairs = groups * pairs_here
+    heads = attn.shape[2]
+    feats = resid.shape[2]
+    block = w_out.shape[0] // quarters
+    per = feats // (block * quarters)
+    place = d * quarters + m
+
+    rows_a = lax.all_gather(attn.reshape(rows_here, heads), "dp", axis=0, tiled=True)
+    moved = lax.all_to_all(
+        resid.reshape(rows_here, per, quarters, block), "mp", split_axis=2, concat_axis=2, tiled=True
+    )
+    moved = moved.transpose(2, 1, 0, 3).reshape(groups, rows_here, block)
+    moved = lax.all_to_all(moved, "dp", split_axis=0, concat_axis=0, tiled=True)
+    gain_all = lax.all_gather(gain, "mp", axis=0, tiled=True)
+    gain_here = lax.dynamic_slice(gain_all, (place * block,), (block,))
+
+    proj_part = lax.dot_general(
+        rows_a, w_out, (((1,), (1,)), ((), ())), preferred_element_type=jnp.float32
+    )
+    proj = lax.psum_scatter(proj_part, "mp", scatter_dimension=1, tiled=True)
+    hidden = moved.reshape(groups * rows_here, block).astype(jnp.float32) + proj
+    normed = hidden * gain_here
+    split = (groups, 2, pairs_here, block)
+    rough = normed.astype(jnp.bfloat16).reshape(split)
+    dots_part = lax.dot_general(
+        rough[:, 0].reshape(pairs, block),
+        rough[:, 1].reshape(pairs, block),
+        (((1,), (1,)), ((), ())),
+        preferred_element_type=jnp.float32,
+    )
+    dots = lax.psum_scatter(dots_part, ("dp", "mp"), scatter_dimension=0, tiled=True)
+    squares = lax.psum(jnp.sum(normed * normed, axis=1), ("dp", "mp"))
+    recip = lax.rsqrt(squares + EPS)
+    recip_split = recip.reshape(groups, 2, pairs_here)
+
+    queries = pairs // (groups * quarters)
+    recip_q = lax.dynamic_slice(recip_split[:, 0].reshape(pairs), (place * queries,), (queries,))
+    recip_e = recip_split[:, 1].reshape(pairs)
+    cosine = dots * recip_q[:, None] * recip_e[None, :]
+    ids = neg_owner * pairs_here + neg_local
+    ids = lax.dynamic_slice(ids, (m * queries, 0), (queries, ids.shape[1]))
+    column = jnp.arange(pairs, dtype=jnp.int32)
+    own = (place * queries + jnp.arange(queries, dtype=jnp.int32))[:, None] == column[None, :]
+    own = own.astype(jnp.float32)
+    times = own + jnp.sum((ids[:, :, None] == column).astype(jnp.float32), axis=1)
+    expo = times * jnp.exp(cosine / TAU)
+    prob = expo / jnp.sum(expo, axis=1, keepdims=True)
+    wts = LOSS_SCALE * (prob - own) / TAU
+    along = wts * cosine
+    along_q = jnp.pad(jnp.sum(along, axis=1)[None, :], ((0, 0), (0, pairs - queries)))
+    along_e = jnp.sum(along, axis=0)[None, :]
+    packed = jnp.concatenate([wts, along_q, along_e], axis=0)
+    packed = jnp.pad(packed, ((0, -packed.shape[0] % 8), (0, 0)))
+    packed = lax.all_gather(packed, ("dp", "mp"), axis=0)
+    wts_all = packed[:, :queries].reshape(pairs, pairs).astype(jnp.bfloat16)
+    along_q = packed[:, queries, :queries].reshape(groups, 1, pairs_here)
+    along_e = jnp.sum(packed[:, queries + 1], axis=0).reshape(groups, 1, pairs_here)
+    along_all = jnp.concatenate([along_q, along_e], axis=1).reshape(-1, 1)
+
+    recip = recip[:, None]
+    unit = normed * recip
+    emb = unit.astype(jnp.bfloat16).reshape(split)
+    grad_q = jnp.dot(
+        wts_all, emb[:, 1].reshape(pairs, block), preferred_element_type=jnp.float32
+    )
+    grad_e = lax.dot_general(
+        wts_all,
+        emb[:, 0].reshape(pairs, block),
+        (((0,), (0,)), ((), ())),
+        preferred_element_type=jnp.float32,
+    )
+    one = (groups, 1, pairs_here, block)
+    demb = jnp.concatenate([grad_q.reshape(one), grad_e.reshape(one)], axis=1).reshape(-1, block)
+    dnorm = recip * (demb - unit * along_all)
+    gain_grad = lax.all_gather(jnp.sum(dnorm * hidden, axis=0), ("dp", "mp"), axis=0, tiled=True)
+    gain_grad = lax.dynamic_slice(gain_grad, (m * feats,), (feats,))
+    dh = (dnorm * gain_here).astype(jnp.bfloat16)
+    dh_full = lax.all_gather(dh, "mp", axis=1, tiled=True)
+    attn_part = jnp.dot(dh_full, w_out, preferred_element_type=jnp.float32)
+    attn_grad = lax.psum_scatter(attn_part, "dp", scatter_dimension=0, tiled=True)
+    attn_grad = attn_grad.astype(jnp.bfloat16).reshape(attn.shape)
+    weight_grad = lax.dot_general(
+        dh_full, rows_a, (((0,), (0,)), ((), ())), preferred_element_type=jnp.float32
+    )
+    return (attn_grad, weight_grad, gain_grad)
+
+
+def shards(attn, resid, w_out, gain, neg_owner, neg_local):
+    groups, quarters = lax.axis_size("dp"), lax.axis_size("mp")
+    block = w_out.shape[0] // quarters
+    fits = block % 128 == 0 and resid.shape[2] % (block * quarters) == 0
+    fits = fits and groups * attn.shape[1] <= 1024 and attn.shape[1] % quarters == 0
+    plan = by_feature if fits else by_query
+    return plan(attn, resid, w_out, gain, neg_owner, neg_local)
+
+
 def solution(mesh):
     in_specs = (
         P(None, "dp", "mp"),

time: 762 us -> 423 us (0.56)
  waiting for transfers between devices: 564 us -> 286 us
  local copies, waits for them, and re-layouts: 56.9 us -> 5.86 us
  blocking collectives: 53.4 us -> 93.5 us
  other arithmetic: 36.4 us -> 8.58 us
  matrix products: 25.5 us -> 10.2 us
    all_to_all x2 -> x1, waiting for transfers between devices: 340 us -> 3.44 us  [by_feature(): moved = lax.all_to_all(moved, 'dp', split_axis=0, concat_axis=0, tiled=True)]
    all_gather x0 -> x2, blocking collectives: none -> 45.5 us  [the longest x1 40.4 us: by_feature(): lax.all_gather(jnp.sum(dnorm * hidden, axis=0), ('dp', 'mp'), axis=0, til...]
    reduce_scatter x2 -> x3, waiting for transfers between devices: 129 us -> 169 us  [the longest x1 135 us: by_feature(): lax.psum_scatter(dots_part, ('dp', 'mp'), scatter_dimension=0, tiled=True)]
    gather x2 -> x0, local copies, waits for them, and re-layouts: 28.6 us -> none  [the longest x1 15.3 us: shards(): fetched.reshape(groups * capacity, feats)[slot]]
    scatter x1 -> x0, other arithmetic: 22.3 us -> none  [shards(): jnp.zeros((groups * capacity, feats), jnp.bfloat16).at[slot]]
    all_gather x2 -> x3, waiting for transfers between devices: 94.4 us -> 113 us  [the longest x1 51.6 us: by_feature(): packed = lax.all_gather(packed, ('dp', 'mp'), axis=0)]
    dot_general x6, matrix products: 25.5 us -> 10.2 us  [the longest x1 3.37 us: by_feature(): attn_part = jnp.dot(dh_full, w_out, preferred_element_type=jnp.float32)]
    mul x5 -> x2, local copies, waits for them, and re-layouts: 11.8 us -> 0.16 us  [the longest x1 0.08 us: by_feature(): dnorm = recip * (demb - unit * along_all)]
  transfers between devices with their start and end apart: 6 -> 7, of which waited for: 6 -> 7; matrix products, arithmetic and copies ran while one was open for 4% -> 1% of each run, Pallas kernels for 0% -> 0%
where the time goes in v1:
time: 423 us; the launch traced here: 422 us
  waiting for transfers between devices  286 us (68%)
  blocking collectives  93.5 us (22%)
  between operations  14.3 us (3%)
  matrix products  10.2 us (2%)
  other arithmetic  8.58 us (2%)
  local copies, waits for them, and re-layouts  5.86 us (1%)
    reduce_scatter x1, waiting for transfers between devices, by_feature(): lax.psum_scatter(dots_part, ('dp', 'mp'), scatter_dimension=0, tiled=True)  135 us
    all_gather x1, waiting for transfers between devices, by_feature(): packed = lax.all_gather(packed, ('dp', 'mp'), axis=0)  51.6 us
    all_gather x1, waiting for transfers between devices, by_feature(): lax.all_gather(attn.reshape(rows_here, heads), 'dp', axis=0, tiled=True)  45.1 us
    all_gather x1, blocking collectives, by_feature(): lax.all_gather(jnp.sum(dnorm * hidden, axis=0), ('dp', 'mp'), axis=0, til...  40.4 us
    psum x1, blocking collectives, by_feature(): squares = lax.psum(jnp.sum(normed * normed, axis=1), ('dp', 'mp'))  39.4 us
    reduce_scatter x1, waiting for transfers between devices, by_feature(): lax.psum_scatter(attn_part, 'dp', scatter_dimension=0, tiled=True)  25.8 us
    all_gather x1, waiting for transfers between devices, by_feature(): dh_full = lax.all_gather(dh, 'mp', axis=1, tiled=True)  15.8 us
    all_to_all x1, blocking collectives, by_feature(): lax.all_to_all(resid.reshape(rows_here, per, quarters, block), 'mp', spli...  8.58 us
  transfers between devices with their start and end apart: 7, of which 7 were waited for; matrix products, arithmetic and copies ran while one was open for 1% of the time, Pallas kernels for 0%

profile of v1, /device:TPU:0, one launch (start us, length us, event | category | flops | bytes accessed | tf_op | source)
XLA Modules:
  0.0 422.1 jit_solution(15479046425597211830)
XLA Ops:
  7.2 0.7 all-gather.6.cloned.1.call-update
  8.0 45.1 %all-gather.6.cloned.1.call-done = bf16[1024,512]{1,0:T(8,128)(2,1)} async-done(((bf16[128,512]{1,0:T(8,128)(2,1)}), bf16[1024,512]{1,0:T(8,128)(2,1)}) %all-gather.6.cloned.1.call-update) | async-done | bytes 1048592 | tf_op jit(solution)/shard_map/all_gather | solution.py:104
  53.0 3.3 fusion.12
  56.8 8.6 %all_to_all.10 = bf16[128,2,4,128]{3,1,0,2:T(2,128)(2,1)S(1)} all-to-all(bf16[128,2,4,128]{3,1,0,2:T(2,128)(2,1)S(1)} %copy.31), channel_id=1, replica_groups=mesh['dp'=8,'mp'=4] {'mp'}, dimensions={2} | all-to-all | bytes 524288 | tf_op jit(solution)/shard_map/all_to_all | solution.py:105
  65.3 0.7 copy.32
  66.1 3.4 all-to-all-start.1
  69.6 5.2 %all_gather.19 = f32[4096]{0:T(1024)S(1)} all-gather(f32[1024]{0:T(1024)S(1)} %copy-done.7), channel_id=1, replica_groups=mesh['dp'=8,'mp'=4] {'mp'}, dimensions={0}, use_global_device_ids=true | all-gather | bytes 20480 | tf_op jit(solution)/shard_map/all_gather | solution.py:110
  74.8 3.4 all-to-all-done.1
  78.3 8.4 %reduce-scatter.4.cloned.1.call-done = f32[1024,128]{1,0:T(8,128)} async-done(((f32[1024,512]{1,0:T(8,128)}), f32[1024,128]{1,0:T(8,128)}) %reduce-scatter.4.cloned.1.call-update) | async-done | bytes 524304 | tf_op jit(solution)/shard_map/reduce_scatter | solution.py:116
  86.7 1.3 multiply_reduce_fusion.1
  88.0 39.4 %psum.7 = f32[1024]{0:T(1024)S(1)} all-reduce(f32[1024]{0:T(1024)S(1)} %multiply_reduce_fusion.1), channel_id=1, replica_groups=mesh['dp'=8,'mp'=4] {'dp','mp'}, use_global_device_ids=true, to_apply=%region_2.0 | all-reduce | flops 1024 | bytes 8192 | tf_op jit(solution)/shard_map/psum | solution.py:128
  127.4 1.3 multiply_convert_fusion.1
  128.7 1.3 fusion.13
  130.6 135.0 %reduce-scatter.6.cloned.1.call-done = f32[16,512]{1,0:T(8,128)} async-done(((f32[512,512]{1,0:T(8,128)}), f32[16,512]{1,0:T(8,128)}) %reduce-scatter.6.cloned.1.call-update) | async-done | bytes 32784 | tf_op jit(solution)/shard_map/reduce_scatter | solution.py:127
  265.6 1.0 fusion.8
  266.6 1.0 fusion.6
  267.5 0.6 pad.9
  268.3 51.6 %all-gather.10.cloned.1.call-done = f32[768,512]{1,0:T(8,128)} async-done(((f32[24,512]{1,0:T(8,128)}), f32[768,512]{1,0:T(8,128)}) %all-gather.10.cloned.1.call-update) | async-done | bytes 1572880 | tf_op jit(solution)/shard_map/all_gather | solution.py:150
  319.9 1.1 slice_reduce_fusion
  321.0 0.9 slice.43
  321.9 1.3 slice.49
  323.7 0.3 convolution_bitcast_fusion.1
  324.0 0.3 convolution_bitcast_fusion
  324.4 0.3 copy-done.1
  324.8 1.0 multiply_reduce_fusion
  325.9 15.8 %all-gather.8.cloned.1.call-done = bf16[1024,512]{1,0:T(8,128)(2,1)} async-done(((bf16[1024,128]{1,0:T(8,128)(2,1)}), bf16[1024,512]{1,0:T(8,128)(2,1)}) %all-gather.8.cloned.1.call-update) | async-done | bytes 1048592 | tf_op jit(solution)/shard_map/all_gather | solution.py:174
  341.7 3.4 fusion.14
  345.1 40.4 %all-gather.1 = f32[32,1,128]{2,1,0:T(1,128)S(1)} all-gather(f32[1,1,128]{2,1,0:T(1,128)S(1)} %bitcast.83), channel_id=1, replica_groups=mesh['dp'=8,'mp'=4] {'dp','mp'}, dimensions={0}, use_global_device_ids=true | all-gather | bytes 16896 | tf_op jit(solution)/shard_map/all_gather | solution.py:171
  385.5 0.6 dynamic_slice.15
  386.1 1.7 fusion.15
  387.8 25.8 %reduce-scatter.8.cloned.1.call-done = f32[128,512]{1,0:T(8,128)} async-done(((f32[1024,512]{1,0:T(8,128)}), f32[128,512]{1,0:T(8,128)}) %reduce-scatter.8.cloned.1.call-update) | async-done | bytes 262160 | tf_op jit(solution)/shard_map/reduce_scatter | solution.py:176
  413.6 1.6 convert_element_type.45
  (49 shorter events, 2.0 us)
Async XLA Ops:
  7.2 45.9 %copy-start = (bf16[512,512]{1,0:T(8,128)(2,1)S(1)}, bf16[512,512]{1,0:T(8,128)(2,1)}, u32[]{:S(2)}) copy-start(bf16[512,512]{1,0:T(8,128)(2,1)} %param.8) | copy-start | bytes 1572868
  7.2 45.8 %all-gather.6.cloned.1.call-start = ((), (), s32[]{:S(2)}) async-start(), calls=%async_computation.5 | async-start | bytes 1179648 | tf_op jit(solution)/shard_map/all_gather | solution.py:104
  7.9 48.5 %copy-start.4 = (bf16[2,64,1024]{2,1,0:T(8,128)(2,1)S(1)}, bf16[2,64,1024]{2,1,0:T(8,128)(2,1)}, u32[]{:S(2)}) copy-start(bf16[2,64,1024]{2,1,0:T(8,128)(2,1)} %param.7) | copy-start | bytes 786436
  7.9 78.8 %reduce-scatter.4.cloned.1.call-start = ((), (), s32[]{:S(2)}) async-start(), calls=%async_computation.6 | async-start | bytes 2621440 | tf_op jit(solution)/shard_map/reduce_scatter | solution.py:116
  56.3 13.2 %copy-start.7 = (f32[1024]{0:T(1024)S(1)}, f32[1024]{0:T(1024)}, u32[]{:S(2)}) copy-start(f32[1024]{0:T(1024)} %param.9) | copy-start | bytes 12292
  66.1 12.2 %all-to-all-start.1 = ((bf16[8,128,128]{2,1,0:T(8,128)(2,1)}), bf16[8,128,128]{2,1,0:T(8,128)(2,1)S(1)}, u32[]{:S(2)}, u32[]{:S(2)}) async-start(bf16[8,128,128]{2,1,0:T(8,128)(2,1)} %bitcast.1), calls=%async_computation.1 | async-start | bytes 524288 | tf_op jit(solution)/shard_map/all_to_all | solution.py:109
  69.5 196.1 %reduce-scatter.6.cloned.1.call-start = ((), (), s32[]{:S(2)}) async-start(), calls=%async_computation.7 | async-start | bytes 1081344 | tf_op jit(solution)/shard_map/reduce_scatter | solution.py:127
  127.4 2.7 copy-start.5
  127.4 2.7 copy-start.6
  130.0 189.9 %all-gather.10.cloned.1.call-start = ((), (), s32[]{:S(2)}) async-start(), calls=%async_computation.10 | async-start | bytes 1622016 | tf_op jit(solution)/shard_map/all_gather | solution.py:150
  268.2 73.5 %all-gather.8.cloned.1.call-start = ((), (), s32[]{:S(2)}) async-start(), calls=%async_computation.8 | async-start | bytes 1310720 | tf_op jit(solution)/shard_map/all_gather | solution.py:174
  323.7 1.0 copy-start.1
  325.8 60.2 %copy-start.2 = (bf16[1024,512]{1,0:T(8,128)(2,1)S(1)}, bf16[1024,512]{1,0:T(8,128)(2,1)}, u32[]{:S(2)}) copy-start(bf16[1024,512]{1,0:T(8,128)(2,1)} %all-gather.6.cloned.1.call-done) | copy-start | bytes 3145732
  325.8 87.7 %reduce-scatter.8.cloned.1.call-start = ((), (), s32[]{:S(2)}) async-start(), calls=%async_computation.9 | async-start | bytes 2359296 | tf_op jit(solution)/shard_map/reduce_scatter | solution.py:176
  341.7 44.4 %copy-start.3 = (bf16[1024,512]{1,0:T(8,128)(2,1)S(1)}, bf16[1024,512]{1,0:T(8,128)(2,1)}, u32[]{:S(2)}) copy-start(bf16[1024,512]{1,0:T(8,128)(2,1)} %all-gather.8.cloned.1.call-done) | copy-start | bytes 3145732
Sparse Core Ops, SparseCore 0:
  10.1 42.8 all-gather.5
  56.5 30.1 reduce-scatter.3
  130.1 135.4 reduce-scatter.5
  268.9 50.9 all-gather.9
  326.0 15.7 all-gather.7
  345.2 68.3 reduce-scatter.7
